TPU v7x, 1024 devices: a whole 4x4x32 slice. The times are simulated.
1024 devices in a mesh: fsdp: 32 (over z), head: 8 (over x, core), rep: 4 (over y).
Axes of the slice: x: 4, y: 4, z: 32, core: 2. Of those that a mesh axis runs over, the one named last changes fastest.
Arguments:
- expert_master: float32 [32, 7168, 2048], P(None, ('rep', 'fsdp'), 'head'), may hold values from -0.0625 to 0.0625
- placement: int32 [32], replicated, may hold values from 0 to 31, as said below
- hidden_rows: bfloat16 [512, 7168], P(None, 'rep'), may hold values from -6 to 6
- routes: int32 [512, 8], replicated, may hold values from 0 to 31, all different within a row
- route_weight: float32 [512, 8], replicated, may hold values from 0.1 to 1
- att_master: float32 [512, 64, 256], P(('fsdp', 'head')), may hold values from -0.5 to 0.5
- query_nope: bfloat16 [4, 512, 64, 128], P(None, ('fsdp', 'rep'), 'head'), may hold values from -6 to 6
- query_rope: bfloat16 [4, 512, 64, 64], P(None, ('fsdp', 'rep'), 'head'), may hold values from -250 to 250
- cache_latent: bfloat16 [512, 512, 576], P(('fsdp', 'rep')), may hold values from -4.1 to 4.1
- cache_len: int32 [512], P(('fsdp', 'rep')), may hold values from 2 to 512, as said below
- new_latent: bfloat16 [4, 512, 576], P(None, ('fsdp', 'rep')), may hold values from -4 to 4
Outputs:
- expert_hidden: bfloat16 [64, 512, 2048], P('fsdp', 'rep', 'head')
- attention_out: bfloat16 [4, 512, 8192], P(None, ('fsdp', 'rep'), 'head')
Inputs may be any that keep to these rules, and one draw needn't show every extreme that they name: `placement`: each owner holds at most 2 experts, and some owner holds exactly 2. `cache_len`: row 0 uses every position.
All inputs are finite; a program needn't handle non-finite values.
Results may differ from a plain program's by a relative error of at most 0.0081.
Values may be sent and summed in bfloat16 or wider, within the bound.
A program may use at most 64 MiB of HBM per device.

v0:
```python
import math

import jax
import jax.numpy as jnp
from jax import lax
from jax.sharding import PartitionSpec as P

LAT = 512
HDIM = 128
SLOTS = 2


def local(
    expert_master,
    placement,
    hidden_rows,
    routes,
    route_weight,
    att_master,
    query_nope,
    query_rope,
    cache_latent,
    cache_len,
    new_latent,
):
    owners = lax.axis_size("fsdp")
    count = placement.shape[0]
    expert_ids = jnp.arange(count, dtype=jnp.int32)
    same = placement[:, None] == placement[None, :]
    earlier = expert_ids[None, :] < expert_ids[:, None]
    slot_of = jnp.sum((same & earlier).astype(jnp.int32), axis=1)
    owner_ids = jnp.arange(owners, dtype=jnp.int32)
    slot_ids = jnp.arange(SLOTS, dtype=jnp.int32)
    match = (slot_ids[:, None, None] == slot_of[None, None, :]) & (
        owner_ids[None, :, None] == placement[None, None, :]
    )
    picked = jnp.sum(jnp.where(match, expert_ids[None, None, :], 0), axis=2)
    filled = jnp.any(match, axis=2)
    row_count = expert_master.shape[1]
    unit_count = expert_master.shape[2]
    mine = lax.axis_index("fsdp")
    share_rows = hidden_rows.shape[0] // lax.axis_size("rep")
    first_row = lax.axis_index("rep") * share_rows
    blocks = jnp.take(expert_master, picked.reshape(-1), axis=0).astype(jnp.bfloat16)
    blocks = blocks.reshape(SLOTS, owners, row_count, unit_count)
    outgoing = jnp.where(filled[:, :, None, None], blocks, jnp.zeros_like(blocks))
    arrived = lax.all_to_all(outgoing, "fsdp", split_axis=1, concat_axis=1, tiled=True)
    weights_here = arrived.reshape(SLOTS, owners * row_count, unit_count)
    my_experts = lax.dynamic_index_in_dim(picked, mine, 1, keepdims=False)
    my_filled = lax.dynamic_index_in_dim(filled, mine, 1, keepdims=False)
    terms = jnp.einsum("rd,sdf->srf", hidden_rows, weights_here, preferred_element_type=jnp.float32)
    hits = routes[None, :, :] == my_experts[:, None, None]
    gate = jnp.sum(jnp.where(hits, route_weight[None, :, :], 0.0), axis=2)
    gate = jnp.where(my_filled[:, None], gate, 0.0)
    summed = lax.psum(terms, "rep")
    share = lax.dynamic_slice_in_dim(summed, first_row, share_rows, 1)
    gate_share = lax.dynamic_slice_in_dim(gate, first_row, share_rows, 1)
    activated = (jax.nn.silu(share) * gate_share[:, :, None]).astype(jnp.bfloat16)
    local_maps = att_master.astype(jnp.bfloat16)[None]
    widened = lax.all_gather(local_maps, "fsdp", axis=0, tiled=True)
    spread = lax.all_to_all(widened[:, None], "head", split_axis=3, concat_axis=1, tiled=True)
    maps = spread.reshape(-1, spread.shape[3], spread.shape[4])
    key_map = maps[:, :, :HDIM]
    value_map = maps[:, :, HDIM:]
    q_latent = jnp.einsum(
        "trhd,lhd->trhl", query_nope, key_map, preferred_element_type=jnp.float32
    ).astype(jnp.bfloat16)
    query_full = jnp.concatenate([q_latent, query_rope], axis=3)
    scale = 1.0 / math.sqrt(query_nope.shape[3] + query_rope.shape[3])
    old_scores = (
        jnp.einsum("trhc,rjc->trhj", query_full, cache_latent, preferred_element_type=jnp.float32)
        * scale
    )
    new_scores = (
        jnp.einsum("trhc,urc->trhu", query_full, new_latent, preferred_element_type=jnp.float32)
        * scale
    )
    positions = jnp.arange(cache_latent.shape[1], dtype=jnp.int32)
    live = positions[None, :] < cache_len[:, None]
    old_scores = jnp.where(live[None, :, None, :], old_scores, -1e30)
    step_ids = jnp.arange(new_latent.shape[0], dtype=jnp.int32)
    causal = step_ids[None, :] <= step_ids[:, None]
    new_scores = jnp.where(causal[:, None, None, :], new_scores, -1e30)
    highest = jnp.maximum(jnp.max(old_scores, axis=3), jnp.max(new_scores, axis=3))
    old_exp = jnp.exp(old_scores - highest[..., None])
    new_exp = jnp.exp(new_scores - highest[..., None])
    total = jnp.sum(old_exp, axis=3) + jnp.sum(new_exp, axis=3)
    old_probs = (old_exp / total[..., None]).astype(jnp.bfloat16)
    new_probs = (new_exp / total[..., None]).astype(jnp.bfloat16)
    latent_full = jnp.einsum(
        "trhj,rjc->trhc", old_probs, cache_latent, preferred_element_type=jnp.float32
    )
    latent_full = latent_full + jnp.einsum(
        "trhu,urc->trhc", new_probs, new_latent, preferred_element_type=jnp.float32
    )
    latent_out = latent_full[..., :LAT].astype(jnp.bfloat16)
    attention = jnp.einsum(
        "trhl,lhv->trhv", latent_out, value_map, preferred_element_type=jnp.float32
    ).astype(jnp.bfloat16)
    attention_out = attention.reshape(
        attention.shape[0], attention.shape[1], attention.shape[2] * attention.shape[3]
    )
    return (activated, attention_out)


def solution(mesh):
    placed = (
        P(None, ("rep", "fsdp"), "head"),
        P(),
        P(None, "rep"),
        P(),
        P(),
        P(("fsdp", "head"), None, None),
        P(None, ("fsdp", "rep"), "head", None),
        P(None, ("fsdp", "rep"), "head", None),
        P(("fsdp", "rep"), None, None),
        P(("fsdp", "rep")),
        P(None, ("fsdp", "rep"), None),
    )
    return jax.shard_map(
        local,
        mesh=mesh,
        in_specs=placed,
        out_specs=(P("fsdp", "rep", "head"), P(None, ("fsdp", "rep"), "head")),
        check_vma=False,
    )
```

profile of v0, /device:TPU:8, one launch (start us, length us, event | category | flops | bytes accessed | tf_op | source)
XLA Modules:
  0.0 460.6 jit_solution(17678214736870443839)
XLA Ops:
  8.0 0.0 copy-start
  8.0 0.0 all-gather.3.cloned.1.call-start
  8.1 1.7 convert_element_type.35
  9.8 0.0 all-gather.3.cloned.1.call-update
  9.8 149.2 %all-gather.3.cloned.1.call-done = bf16[64,64,256]{2,1,0:T(8,128)(2,1)} async-done(((bf16[2,64,256]{2,1,0:T(8,128)(2,1)}), bf16[64,64,256]{2,1,0:T(8,128)(2,1)}) %all-gather.3.cloned.1.call-update) | async-done | bytes 2097168 | tf_op jit(solution)/shard_map/all_gather | solution.py:60
  159.0 5.0 %copy.94 = bf16[32,1,2,64,256]{4,2,0,1,3:T(2,128)(2,1)} copy(bf16[32,1,2,64,256]{4,3,2,0,1:T(8,128)(2,1)} %bitcast.69) | data formatting | bytes 4194304 | tf_op jit(solution)/shard_map/broadcast_in_dim | solution.py:61
  164.1 0.0 copy-start.6
  164.1 4.5 all-to-all-start.1
  168.5 0.0 copy-done.6
  168.5 0.2 convert_reduce_fusion
  168.7 0.1 fusion.38
  168.9 0.1 reshape.147
  169.0 3.5 gather_fusion
  172.5 0.1 and_reduce_fusion
  172.6 2.0 fusion.4
  174.6 1.4 copy.91
  176.0 0.0 copy-start.2
  176.0 0.0 copy-start.4
  176.0 0.0 copy-start.5
  176.0 0.0 copy-start.7
  176.0 19.7 %all-to-all-done.1 = bf16[32,1,2,64,256]{4,2,0,1,3:T(2,128)(2,1)} async-done(((bf16[32,1,2,64,256]{4,2,0,1,3:T(2,128)(2,1)}), bf16[32,1,2,64,256]{4,2,0,1,3:T(2,128)(2,1)}, u32[]{:S(2)}, u32[]{:S(2)}) %all-to-all-start.1) | async-done | bytes 2097184 | tf_op jit(solution)/shard_map/all_to_all | solution.py:61
  195.7 12.2 %all-to-all-start = ((bf16[2,32,56,256]{3,2,0,1:T(8,128)(2,1)}), bf16[2,32,56,256]{3,2,0,1:T(8,128)(2,1)}, u32[]{:S(2)}, u32[]{:S(2)}) async-start(bf16[2,32,56,256]{3,2,0,1:T(8,128)(2,1)} %copy.91), calls=%async_computation | async-start | bytes 3670016 | tf_op jit(solution)/shard_map/all_to_all | solution.py:47
  207.9 0.2 all-reduce.2.cloned.1.call-start
  208.1 0.2 dynamic-slice_reduce_fusion.1
  208.3 0.2 dynamic-slice_reduce_fusion
  208.5 0.0 copy-done.2
  208.6 0.0 copy-done.4
  208.6 0.0 copy-done.5
  208.6 0.1 select_reduce_fusion
  208.7 0.1 dynamic-slice_select_fusion
  208.7 0.0 copy-done.7
  208.7 0.1 iota_compare_fusion.2
  208.8 3.3 copy.137
  212.1 3.5 copy.96
  215.6 0.0 copy-start.9
  215.6 4.1 reshape.149
  219.7 0.0 copy-done.9
  219.7 1.7 fusion.28
  221.4 0.1 pad_maximum_fusion
  221.5 0.0 copy-done
  221.5 0.6 fusion.48
  222.0 156.3 %all-to-all-done = bf16[2,32,56,256]{3,2,0,1:T(8,128)(2,1)} async-done(((bf16[2,32,56,256]{3,2,0,1:T(8,128)(2,1)}), bf16[2,32,56,256]{3,2,0,1:T(8,128)(2,1)}, u32[]{:S(2)}, u32[]{:S(2)}) %all-to-all-start) | async-done | bytes 1835040 | tf_op jit(solution)/shard_map/all_to_all | solution.py:47
  378.3 0.0 copy-start.8
  378.3 1.8 copy.92
  380.1 0.3 copy-done.8
  380.4 0.0 copy-start.3
  380.4 2.1 fusion.7
  382.5 0.0 all-reduce.2.cloned.1.call-update
  382.6 0.0 copy-done.3
  382.6 0.6 fusion.49
  383.2 0.2 fusion.32
  383.4 0.0 copy-start.1
  383.4 0.2 fusion.41
  383.7 0.8 fusion.25
  384.5 0.5 copy-done.1
  385.0 0.3 fusion.29
  385.3 0.6 copy.138
  385.9 65.5 %all-reduce.2.cloned.1.call-done = f32[2,512,256]{1,2,0:T(8,128)} async-done(((f32[2,512,256]{1,2,0:T(8,128)}), f32[2,512,256]{1,2,0:T(8,128)}) %all-reduce.2.cloned.1.call-update) | async-done | bytes 1048592 | tf_op jit(solution)/shard_map/psum | solution.py:55
  451.4 1.0 multiply_convert_fusion
  452.4 0.8 copy.105
  (11 shorter events, 0.1 us)
Async XLA Ops:
  8.0 213.5 %copy-start = (bf16[4,512,576]{1,2,0:T(8,128)(2,1)S(1)}, bf16[4,512,576]{1,2,0:T(8,128)(2,1)}, u32[]{:S(2)}) copy-start(bf16[4,512,576]{1,2,0:T(8,128)(2,1)} %param.19) | copy-start | bytes 7077892
  8.0 151.0 %all-gather.3.cloned.1.call-start = ((), (), s32[]{:S(2)}) async-start(), calls=%async_computation.3 | async-start | bytes 2162688 | tf_op jit(solution)/shard_map/all_gather | solution.py:60
  164.1 4.5 copy-start.6
  164.1 31.7 %all-to-all-start.1 = ((bf16[32,1,2,64,256]{4,2,0,1,3:T(2,128)(2,1)}), bf16[32,1,2,64,256]{4,2,0,1,3:T(2,128)(2,1)}, u32[]{:S(2)}, u32[]{:S(2)}) async-start(bf16[32,1,2,64,256]{4,2,0,1,3:T(2,128)(2,1)} %copy.94), calls=%async_computation.1 | async-start | bytes 4194304 | tf_op jit(solution)/shard_map/all_to_all | solution.py:61
  176.0 32.5 %copy-start.2 = (bf16[4,4,8,64]{3,2,1,0:T(8,128)(2,1)S(1)}, bf16[4,4,8,64]{3,2,1,0:T(8,128)(2,1)}, u32[]{:S(2)}) copy-start(bf16[4,4,8,64]{3,2,1,0:T(8,128)(2,1)} %param.18) | copy-start | bytes 49156
  176.0 32.6 %copy-start.4 = (f32[512,8]{0,1:T(8,128)S(1)}, f32[512,8]{0,1:T(8,128)}, u32[]{:S(2)}) copy-start(f32[512,8]{0,1:T(8,128)} %param.15) | copy-start | bytes 49156
  176.0 32.6 %copy-start.5 = (s32[512,8]{0,1:T(8,128)S(1)}, s32[512,8]{0,1:T(8,128)}, u32[]{:S(2)}) copy-start(s32[512,8]{0,1:T(8,128)} %param.14) | copy-start | bytes 49156
  176.0 32.7 %copy-start.7 = (s32[4]{0:T(128)S(1)}, s32[4]{0:T(128)}, u32[]{:S(2)}) copy-start(s32[4]{0:T(128)} %param.20) | copy-start | bytes 52
  195.7 182.6 %all-to-all-start = ((bf16[2,32,56,256]{3,2,0,1:T(8,128)(2,1)}), bf16[2,32,56,256]{3,2,0,1:T(8,128)(2,1)}, u32[]{:S(2)}, u32[]{:S(2)}) async-start(bf16[2,32,56,256]{3,2,0,1:T(8,128)(2,1)} %copy.91), calls=%async_computation | async-start | bytes 3670016 | tf_op jit(solution)/shard_map/all_to_all | solution.py:47
  207.9 243.5 %all-reduce.2.cloned.1.call-start = ((), (), s32[]{:S(2)}) async-start(), calls=%async_computation.2 | async-start | bytes 2097152 | tf_op jit(solution)/shard_map/psum | solution.py:55
  215.6 4.1 copy-start.9
  378.3 2.1 copy-start.8
  380.4 2.2 copy-start.3
  383.4 1.6 copy-start.1
Sparse Core Ops, SparseCore 0:
  12.4 146.5 all-gather.2
Sparse Core Ops, SparseCore 1:
  382.6 68.7 all-reduce.1
where the time goes:
time: 461 us
  waiting for transfers between devices  391 us (85%)
  local copies, waits for them, and re-layouts  25.3 us (5%)
  starting transfers between devices  16.9 us (4%)
  between operations  15.7 us (3%)
  matrix products  6.26 us (1%)
  other arithmetic  5.75 us (1%)
    all_to_all x1, waiting for transfers between devices, local(): lax.all_to_all(outgoing, 'fsdp', split_axis=1, concat_axis=1, tiled=True)  156 us
    all_gather x1, waiting for transfers between devices, local(): widened = lax.all_gather(local_maps, 'fsdp', axis=0, tiled=True)  149 us
    psum x1, waiting for transfers between devices, local(): summed = lax.psum(terms, 'rep')  65.5 us
    all_to_all x1, waiting for transfers between devices, local(): lax.all_to_all(widened[:, None], 'head', split_axis=3, concat_axis=1, til...  19.7 us
    all_to_all x1, starting transfers between devices, local(): lax.all_to_all(outgoing, 'fsdp', split_axis=1, concat_axis=1, tiled=True)  12.2 us
  transfers between devices with their start and end apart: 4, of which 4 were waited for; matrix products, arithmetic and copies ran while one was open for 5% of the time, Pallas kernels for 0%

commit v1 on v0

v1 whole, which is shorter than its diff:
```python
import functools
import math

import jax
import jax.numpy as jnp
from jax import lax
from jax.experimental import pallas as pl
from jax.experimental.pallas import tpu as pltpu
from jax.sharding import PartitionSpec as P

MESH = pl.DeviceIdType.MESH
SLOTS = 2
GROUP = 8
F32 = jnp.float32
BF16 = jnp.bfloat16
SPREADS = (3.2, None)


def capacities(n, spread):
    caps = [0]
    for length in range(1, n // 2 + 1):
        cap = 2 * length
        if spread is not None:
            drift = math.sqrt(2 * length * 0.25 * (2 * n - 2 * length) / (2 * n - 1))
            cap = min(cap, int(length + spread * drift))
        caps.append(max(cap, caps[-1], 2))
    return tuple(caps)


class Kind:
    def __init__(self, index, sign, part, reach, caps):
        self.index, self.sign, self.part, self.reach, self.caps = index, sign, part, reach, caps

    def sent(self, hop):
        return self.caps[self.reach - hop + 1]

    def pieces(self, hop):
        if hop < 1 or hop > self.reach:
            return []
        top = self.sent(hop)
        return [(low, min(low + GROUP, top)) for low in range(0, top, GROUP)]


def kinds_of(n, caps):
    half = n // 2
    return (
        Kind(0, 1, 0, half, caps),
        Kind(1, -1, 0, half - 1, caps),
        Kind(2, 1, 1, half - 1, caps),
        Kind(3, -1, 1, half, caps),
    )


def body(
    n,
    heads,
    reps,
    caps,
    tbl,
    lens,
    master_hbm,
    x_hbm,
    gate,
    att,
    qn,
    qr,
    cache_hbm,
    new,
    eh_out,
    at_out,
    *refs,
):
    z, h, y = lax.axis_index("fsdp"), lax.axis_index("head"), lax.axis_index("rep")
    kinds = kinds_of(n, caps)
    bufs = []
    for kind in kinds:
        bufs.append(refs[: kind.reach + 1])
        refs = refs[kind.reach + 1 :]
    (
        master,
        x,
        cache,
        wide_x,
        spread,
        weights,
        landed,
        maps,
        qlat,
        probs,
        latent,
        rs_out,
        rs_in,
        send_sem,
        recv_sem,
        head_send,
        head_recv,
        map_send,
        map_recv,
        y_send,
        y_recv,
        rs_send,
        rs_recv,
        load_sem,
    ) = refs
    half = n // 2
    zn = z + n
    rows = master.shape[1]
    units = master.shape[2]
    lanes = units // 2
    head_rows = rows * 4 // 7
    tail_rows = rows - head_rows
    pad_rows = wide_x.shape[1] // n
    share = x.shape[0] // reps
    local_heads, lat = maps.shape[0], maps.shape[1]
    hdim = maps.shape[2] // 2
    block = lat // n
    z_to = {1: lax.rem(z + 1, n), -1: lax.rem(z + n - 1, n)}
    y_to = {1: lax.rem(y + 1, reps), -1: lax.rem(y + reps - 1, reps)}
    y_far = lax.rem(y + 2, reps)

    loads = [
        pltpu.make_async_copy(master_hbm, master, load_sem.at[0]),
        pltpu.make_async_copy(x_hbm, x, load_sem.at[1]),
        pltpu.make_async_copy(cache_hbm, cache, load_sem.at[2]),
    ]
    for load in loads:
        load.start()

    barrier = pltpu.get_barrier_semaphore()
    for sign in (1, -1):
        pl.semaphore_signal(barrier, inc=1, device_id={"fsdp": z_to[sign]}, device_id_type=MESH)
        pl.semaphore_signal(barrier, inc=1, device_id={"rep": y_to[sign]}, device_id_type=MESH)
    for step in range(1, heads):
        pl.semaphore_signal(
            barrier, inc=1, device_id={"head": lax.rem(h + step, heads)}, device_id_type=MESH
        )
    pl.semaphore_wait(barrier, 4 + heads - 1)

    head_copies = []
    for step in range(1, heads):
        to = lax.rem(h + step, heads)
        copy = pltpu.make_async_remote_copy(
            src_ref=att.at[to],
            dst_ref=landed.at[h],
            send_sem=head_send.at[step],
            recv_sem=head_recv.at[h],
            device_id={"head": to},
            device_id_type=MESH,
        )
        copy.start()
        head_copies.append(copy)

    def head_arrival(step):
        source = lax.rem(h + step, heads)
        return pltpu.make_async_remote_copy(
            src_ref=att.at[source],
            dst_ref=landed.at[source],
            send_sem=head_send.at[step],
            recv_sem=head_recv.at[source],
            device_id={"head": source},
            device_id_type=MESH,
        )

    def map_block(sign, hop):
        owner = lax.rem(zn - sign * hop, n)
        return maps.at[pl.ds(2 * y, 2), pl.ds(pl.multiple_of(owner * block, block), block), :]

    def map_copy(sign, hop):
        index = half * (sign < 0) + hop - 1
        ref = map_block(sign, hop - 1)
        return pltpu.make_async_remote_copy(
            src_ref=ref,
            dst_ref=ref,
            send_sem=map_send.at[index],
            recv_sem=map_recv.at[index],
            device_id={"fsdp": z_to[sign]},
            device_id_type=MESH,
        )

    def map_arrival(sign, hop):
        index = half * (sign < 0) + hop - 1
        ref = map_block(sign, hop)
        return pltpu.make_async_remote_copy(
            src_ref=ref,
            dst_ref=ref,
            send_sem=map_send.at[index],
            recv_sem=map_recv.at[index],
            device_id={"fsdp": z_to[sign]},
            device_id_type=MESH,
        )

    def y_copy(index, sign, low, size):
        ref = maps.at[pl.ds(low, size)]
        return pltpu.make_async_remote_copy(
            src_ref=ref,
            dst_ref=ref,
            send_sem=y_send.at[index],
            recv_sem=y_recv.at[index],
            device_id={"rep": y_to[sign]},
            device_id_type=MESH,
        )

    open_sends = []

    def attention():
        for step in range(1, heads):
            head_arrival(step).wait_recv()
        landed[h] = att[h]
        flat = landed[...].reshape(heads * att.shape[1], att.shape[2]).astype(BF16)
        per = att.shape[1]
        for hq in range(2):
            for side in range(2):
                row = lax.broadcasted_iota(jnp.int32, (block, heads * per), 0)
                col = lax.broadcasted_iota(jnp.int32, (block, heads * per), 1)
                want = (row >> 1) * per + hq * 4 + (row & 1) * 2 + side
                pick = jnp.where(col == want, 1.0, 0.0).astype(BF16)
                piece = jnp.dot(pick, flat, preferred_element_type=F32).astype(BF16)
                maps[
                    2 * y + hq,
                    pl.ds(pl.multiple_of(z * block, block), block),
                    side * hdim : (side + 1) * hdim,
                ] = piece
        for hop in range(1, half + 2):
            for sign in (1, -1):
                top = half if sign > 0 else half - 1
                if 2 <= hop <= top + 1:
                    map_arrival(sign, hop - 1).wait_recv()
                if hop <= top:
                    copy = map_copy(sign, hop)
                    copy.start()
                    open_sends.append(copy)
            yield
        first = [y_copy(0, 1, 2 * y, 2), y_copy(1, -1, 2 * y, 2)]
        for copy in first:
            copy.start()
            open_sends.append(copy)
        for _ in range(5):
            yield
        y_copy(0, 1, 2 * y_to[-1], 2).wait_recv()
        y_copy(1, -1, 2 * y_to[1], 2).wait_recv()
        second = [y_copy(2, 1, 2 * y_to[-1], 1), y_copy(3, -1, 2 * y_to[1] + 1, 1)]
        for copy in second:
            copy.start()
            open_sends.append(copy)
        for _ in range(3):
            yield
        y_copy(2, 1, 2 * y_far, 1).wait_recv()
        y_copy(3, -1, 2 * y_far + 1, 1).wait_recv()
        loads[2].wait()
        yield
        group = qn.shape[0]
        contract = (((1,), (1,)), ((), ()))
        for head in range(local_heads):
            q = qn[:, head * hdim : (head + 1) * hdim]
            qlat[head * group : (head + 1) * group, :] = lax.dot_general(
                q, maps[head, :, :hdim], contract, preferred_element_type=F32
            ).astype(BF16)
        yield
        total_rows = local_heads * group
        count, slots = cache.shape[0], cache.shape[2]
        scale = 1.0 / math.sqrt(hdim + qr.shape[1])
        row = lax.broadcasted_iota(jnp.int32, (total_rows, slots), 0) & (count - 1)
        col = lax.broadcasted_iota(jnp.int32, (total_rows, slots), 1)
        score = jnp.full((total_rows, slots), -1e30, F32)
        for r in range(count):
            part = jnp.dot(qlat[...], cache[r, :lat, :], preferred_element_type=F32) + jnp.dot(
                qr[...], cache[r, lat:, :], preferred_element_type=F32
            )
            score = jnp.where((row == r) & (col < lens[r]), part * scale, score)
        fresh = lax.dot_general(
            qlat[...], new[:, :lat], contract, preferred_element_type=F32
        ) + lax.dot_general(qr[...], new[:, lat:], contract, preferred_element_type=F32)
        nrow = lax.broadcasted_iota(jnp.int32, fresh.shape, 0)
        ncol = lax.broadcasted_iota(jnp.int32, fresh.shape, 1)
        shift = count.bit_length() - 1
        same = (nrow & (count - 1)) == (ncol & (count - 1))
        step_of = (nrow >> shift) & (group // count - 1)
        fresh = jnp.where(same & ((ncol >> shift) <= step_of), fresh * scale, -1e30)
        top = jnp.maximum(
            jnp.max(score, axis=1, keepdims=True), jnp.max(fresh, axis=1, keepdims=True)
        )
        old_exp = jnp.exp(score - top)
        new_exp = jnp.exp(fresh - top)
        total = jnp.sum(old_exp, axis=1, keepdims=True) + jnp.sum(new_exp, axis=1, keepdims=True)
        probs[...] = old_exp / total
        new_probs = (new_exp / total).astype(BF16)
        latent[...] = jnp.dot(new_probs, new[:, :lat], preferred_element_type=F32)
        yield
        for r in range(count):
            mine = jnp.where(row == r, probs[...], 0.0).astype(BF16)
            latent[...] += lax.dot_general(
                mine, cache[r, :lat, :], contract, preferred_element_type=F32
            )
        yield
        for head in range(local_heads):
            lh = latent[head * group : (head + 1) * group, :].astype(BF16)
            at_out[:, head * hdim : (head + 1) * hdim] = jnp.dot(
                lh, maps[head, :, hdim:], preferred_element_type=F32
            ).astype(BF16)

    def widen():
        for slot in range(SLOTS):
            rank = jnp.clip(tbl[0, zn] + slot, 0, tbl.shape[1] - 1)
            expert = jnp.clip(tbl[1, rank], 0, master.shape[0] - 1)
            weights[slot, pl.ds(pl.multiple_of(z * pad_rows, pad_rows), rows), :] = master[
                expert
            ].astype(BF16)
        loads[1].wait()
        yield
        row = lax.broadcasted_iota(jnp.int32, spread.shape, 0)
        col = lax.broadcasted_iota(jnp.int32, spread.shape, 1)
        inside = col & (pad_rows - 1)
        source = col >> (pad_rows.bit_length() - 1)
        spread[...] = jnp.where(
            (inside < rows) & (row == source * rows + inside), 1.0, 0.0
        ).astype(BF16)
        yield
        deep, broad = spread.shape
        for piece in range(x.shape[1] // deep):
            for low in range(0, broad, broad // 2):
                wide_x[:, piece * broad + low : piece * broad + low + broad // 2] = jnp.dot(
                    x[:, piece * deep : (piece + 1) * deep],
                    spread[:, low : low + broad // 2],
                    preferred_element_type=F32,
                ).astype(BF16)
                yield

    def rank_base(kind, source):
        if kind.sign > 0:
            return tbl[0, source + kind.reach + 1] - 1
        return tbl[0, source - kind.reach]

    def assemble(kind, low, high):
        base = rank_base(kind, zn)
        buf = bufs[kind.index][0]

        def one(slot, carry):
            rank = jnp.clip(base - kind.sign * slot, 0, tbl.shape[1] - 1)
            expert = jnp.clip(tbl[1, rank], 0, master.shape[0] - 1)
            if kind.part == 0:
                buf[slot] = master[expert, :head_rows, :].astype(BF16)
            else:
                buf[slot, :tail_rows, :] = master[expert, head_rows:, :lanes].astype(BF16)
                buf[slot, tail_rows:, :] = master[expert, head_rows:, lanes:].astype(BF16)
            return carry

        lax.fori_loop(low, high, one, 0)

    def extract(kind, hop):
        source = zn - kind.sign * hop
        base = rank_base(kind, source)
        buf = bufs[kind.index][hop]
        held = kind.sent(hop)
        row = lax.rem(source, n) * pad_rows
        for slot in range(SLOTS):
            index = kind.sign * (base - (tbl[0, zn] + slot))
            index = jnp.clip(index, 0, held - 1)
            if kind.part == 0:
                weights[slot, pl.ds(pl.multiple_of(row, pad_rows), head_rows), :] = buf[index]
            else:
                at = pl.ds(pl.multiple_of(row + head_rows, head_rows), tail_rows)
                weights[slot, at, :lanes] = buf[index, :tail_rows, :]
                weights[slot, at, lanes:] = buf[index, tail_rows:, :]

    most = -(-max(caps) // GROUP)

    def bundle(kind, hop, piece):
        low, high = kind.pieces(hop)[piece]
        index = (kind.index * half + hop - 1) * most + piece
        return pltpu.make_async_remote_copy(
            src_ref=bufs[kind.index][hop - 1].at[pl.ds(low, high - low)],
            dst_ref=bufs[kind.index][hop].at[pl.ds(low, high - low)],
            send_sem=send_sem.at[index],
            recv_sem=recv_sem.at[index],
            device_id={"fsdp": z_to[kind.sign]},
            device_id_type=MESH,
        )

    loads[0].wait()
    weights[...] = jnp.zeros_like(weights)
    recent = {1: [], -1: []}
    side = [attention()]
    wider = [widen()]

    def ahead(queue):
        if queue:
            try:
                next(queue[0])
            except StopIteration:
                queue.pop()

    for hop in range(1, half + 2):
        for part in range(2):
            pair = [kind for kind in kinds if kind.part == part]
            ticks = max(max(len(k.pieces(hop)), len(k.pieces(hop - 1))) for k in pair)
            for piece in range(ticks):
                for kind in pair:
                    if piece < len(kind.pieces(hop - 1)):
                        bundle(kind, hop - 1, piece).wait_recv()
                    if piece < len(kind.pieces(hop)):
                        if hop == 1:
                            assemble(kind, *kind.pieces(1)[piece])
                            queue = recent[kind.sign]
                            if len(queue) >= 2:
                                queue.pop(0).wait_send()
                            copy = bundle(kind, hop, piece)
                            copy.start()
                            queue.append(copy)
                        else:
                            copy = bundle(kind, hop, piece)
                            copy.start()
                            open_sends.append(copy)
                if hop > 1 or part + piece > 0:
                    ahead(side)
                ahead(wider)
            for kind in pair:
                if 2 <= hop <= kind.reach + 1:
                    extract(kind, hop - 1)
    for source in wider + side:
        for _ in source:
            pass

    def partial(slot, target):
        at = pl.ds(pl.multiple_of(target * share, share), share)
        return jnp.dot(wide_x[at, :], weights[slot], preferred_element_type=F32)

    def rs_copy(index, sign):
        return pltpu.make_async_remote_copy(
            src_ref=rs_out.at[index],
            dst_ref=rs_in.at[index],
            send_sem=rs_send.at[index],
            recv_sem=rs_recv.at[index],
            device_id={"rep": y_to[sign]},
            device_id_type=MESH,
        )

    def send_sum(index, sign, value):
        rs_out[index] = value.astype(BF16)
        copy = rs_copy(index, sign)
        copy.start()
        open_sends.append(copy)

    send_sum(0, 1, partial(0, y_far))
    send_sum(1, -1, partial(1, y_far))
    send_sum(2, 1, partial(1, y_to[1]))
    send_sum(3, -1, partial(0, y_to[-1]))
    up = partial(0, y_to[1])
    rs_copy(0, 1).wait_recv()
    send_sum(4, 1, up + rs_in[0].astype(F32))
    down = partial(1, y_to[-1])
    rs_copy(1, -1).wait_recv()
    send_sum(5, -1, down + rs_in[1].astype(F32))
    own = (partial(0, y), partial(1, y))
    for slot, (index, late, sign) in enumerate(((3, 4, -1), (2, 5, 1))):
        rs_copy(index, sign).wait_recv()
        rs_copy(late, -sign).wait_recv()
        value = own[slot] + rs_in[index].astype(F32) + rs_in[late].astype(F32)
        value = value / (1.0 + jnp.exp(-value))
        for side_of in range(2):
            at = slice(side_of * lanes, (side_of + 1) * lanes)
            eh_out[slot, :, at] = (value[:, at] * gate[slot]).astype(BF16)
    for copy in head_copies + open_sends + recent[1] + recent[-1]:
        copy.wait_send()


def exchange(sizes, caps, collective_id, operands):
    n, heads, reps = sizes
    tbl, lens, master, x, gate, att, qn, qr, cache, new = operands
    experts, rows, units = master.shape
    head_rows = rows * 4 // 7
    pad_rows = 1 << (rows - 1).bit_length()
    kinds = kinds_of(n, caps)
    most = -(-max(caps) // GROUP)
    copies = 4 * (n // 2) * most
    lat = cache.shape[1] - qr.shape[1]
    hdim = att.shape[2]
    total_rows = qr.shape[0]
    local_heads = qn.shape[1] // hdim
    share = x.shape[0] // reps
    group = n
    while group % 2 == 0 and group * rows // 2 % 128 == 0:
        group //= 2
    vmem = pl.BlockSpec(memory_space=pltpu.VMEM)
    smem = pl.BlockSpec(memory_space=pltpu.SMEM)
    hbm = pl.BlockSpec(memory_space=pl.ANY)
    shapes = []
    for kind in kinds:
        block = (head_rows, units) if kind.part == 0 else (2 * (rows - head_rows), units // 2)
        shapes += [(kind.sent(max(hop, 1)), *block) for hop in range(kind.reach + 1)]
    dma = pltpu.SemaphoreType.DMA
    return pl.pallas_call(
        functools.partial(body, n, heads, reps, caps),
        out_shape=(
            jax.ShapeDtypeStruct((SLOTS, share, units), BF16),
            jax.ShapeDtypeStruct(qn.shape, BF16),
        ),
        in_specs=[smem, smem, hbm, hbm, vmem, vmem, vmem, vmem, hbm, vmem],
        out_specs=(vmem, vmem),
        scratch_shapes=[pltpu.VMEM(shape, BF16) for shape in shapes]
        + [
            pltpu.VMEM(master.shape, F32),
            pltpu.VMEM(x.shape, BF16),
            pltpu.VMEM(cache.shape, BF16),
            pltpu.VMEM((x.shape[0], n * pad_rows), BF16),
            pltpu.VMEM((group * rows, group * pad_rows), BF16),
            pltpu.VMEM((SLOTS, n * pad_rows, units), BF16),
            pltpu.VMEM(att.shape, F32),
            pltpu.VMEM((local_heads, lat, 2 * hdim), BF16),
            pltpu.VMEM((total_rows, lat), BF16),
            pltpu.VMEM((total_rows, cache.shape[2]), F32),
            pltpu.VMEM((total_rows, lat), F32),
            pltpu.VMEM((6, share, units), BF16),
            pltpu.VMEM((6, share, units), BF16),
            dma((copies,)),
            dma((copies,)),
            dma((heads,)),
            dma((heads,)),
            dma((n,)),
            dma((n,)),
            dma((4,)),
            dma((4,)),
            dma((6,)),
            dma((6,)),
            dma((3,)),
        ],
        compiler_params=pltpu.CompilerParams(
            collective_id=collective_id,
            has_side_effects=True,
            vmem_limit_bytes=50 * 1024 * 1024,
        ),
    )(*operands)


def local(
    sizes,
    expert_master,
    placement,
    hidden_rows,
    routes,
    route_weight,
    att_master,
    query_nope,
    query_rope,
    cache_latent,
    cache_len,
    new_latent,
):
    n, heads, reps = sizes
    z, y = lax.axis_index("fsdp"), lax.axis_index("rep")
    count = placement.shape[0]
    ids = jnp.arange(count, dtype=jnp.int32)
    width = max(3 * n + 1, 3 * count)
    turns = jnp.arange(3, dtype=jnp.int32) * n
    places = jnp.arange(width, dtype=jnp.int32)
    below = jnp.sum(
        ((placement[None, None, :] + turns[None, :, None]) < places[:, None, None]).astype(jnp.int32),
        axis=(1, 2),
    )
    before = (placement[None, :] < placement[:, None]) | (
        (placement[None, :] == placement[:, None]) & (ids[None, :] < ids[:, None])
    )
    rank = jnp.sum(before.astype(jnp.int32), axis=1)
    ordered = jnp.sum(jnp.where(rank[None, :] == places[:, None] % count, ids[None, :], 0), axis=1)
    tbl = jnp.stack([below, ordered])
    slot_of = jnp.sum(
        ((placement[:, None] == placement[None, :]) & (ids[None, :] < ids[:, None])).astype(jnp.int32), axis=1
    )
    slots = jnp.arange(SLOTS, dtype=jnp.int32)
    here = (placement == z)[None, :] & (slot_of[None, :] == slots[:, None])
    mine = jnp.sum(jnp.where(here, ids[None, :] + 1, 0), axis=1) - 1
    share = hidden_rows.shape[0] // reps
    my_routes = lax.dynamic_slice_in_dim(routes, y * share, share, 0)
    my_weight = lax.dynamic_slice_in_dim(route_weight, y * share, share, 0)
    gate = jnp.sum(jnp.where(my_routes[None] == mine[:, None, None], my_weight[None], 0.0), axis=2)
    units = expert_master.shape[2]
    gate = jnp.broadcast_to(gate[:, :, None], (SLOTS, share, units // 2))

    lat_rows, all_heads, both = att_master.shape
    local_heads = all_heads // heads
    att = att_master.reshape(lat_rows, heads, reps, 2, 2, both // 2)
    att = lax.dynamic_index_in_dim(att, y, 2, keepdims=False)
    att = att.transpose(1, 2, 0, 3, 4).reshape(heads, lat_rows * 4, both // 2)

    steps, rows_here = query_nope.shape[0], query_nope.shape[1]
    group = steps * rows_here
    qn = query_nope.reshape(group, -1)
    qr = query_rope.reshape(group, local_heads, -1).transpose(1, 0, 2).reshape(group * local_heads, -1)
    new = new_latent.reshape(group, -1)
    operands = (tbl, cache_len, expert_master, hidden_rows, gate, att, qn, qr, jnp.swapaxes(cache_latent, 1, 2), new)

    table = [capacities(n, spread) for spread in SPREADS]
    runs = jnp.arange(1, n // 2 + 1, dtype=jnp.int32)
    away = (placement[None, :] - jnp.arange(n, dtype=jnp.int32)[:, None] + n) % n
    held = jnp.sum((away[None] < runs[:, None, None]).astype(jnp.int32), axis=2)
    fullest = jnp.max(held, axis=1)
    tier = jnp.int32(0)
    for caps in table[:-1]:
        over = jnp.any(fullest > jnp.asarray(caps[1:], jnp.int32))
        tier = jnp.where(over & (tier == table.index(caps)), tier + 1, tier)
    branches = [functools.partial(exchange, sizes, caps, index) for index, caps in enumerate(table)]
    hidden, attended = lax.switch(tier, branches, operands)
    return hidden, attended.reshape(steps, rows_here, -1)


def solution(mesh):
    placed = (
        P(None, ("rep", "fsdp"), "head"),
        P(),
        P(None, "rep"),
        P(),
        P(),
        P(("fsdp", "head"), None, None),
        P(None, ("fsdp", "rep"), "head", None),
        P(None, ("fsdp", "rep"), "head", None),
        P(("fsdp", "rep"), None, None),
        P(("fsdp", "rep")),
        P(None, ("fsdp", "rep"), None),
    )
    sizes = (mesh.shape["fsdp"], mesh.shape["head"], mesh.shape["rep"])
    return jax.shard_map(
        functools.partial(local, sizes),
        mesh=mesh,
        in_specs=placed,
        out_specs=(P("fsdp", "rep", "head"), P(None, ("fsdp", "rep"), "head")),
        check_vma=False,
    )
```

time: 461 us -> 193 us (0.42)
  the two profiles are of different devices: /device:TPU:8 before, /device:TPU:32 now
where the time goes in v1:
time: 193 us; the launch traced here: 192 us
  Pallas kernels  180 us (93%)
  local copies, waits for them, and re-layouts  5.61 us (3%)
  other arithmetic  5.48 us (3%)
    pallas_call x1, Pallas kernels, exchange(): pl.pallas_call(functools.partial(body, n, heads, reps, caps), out_shape=(...  180 us

profile of v1, /device:TPU:32, one launch (start us, length us, event | category | flops | bytes accessed | tf_op | source)
XLA Modules:
  0.0 192.3 jit_solution(12604222249839501661)
XLA Ops:
  0.7 0.7 broadcast_add_fusion.2
  1.4 0.1 convert_reduce_fusion.1
  1.5 0.8 fusion.5
  2.3 0.9 convert_reduce_fusion.2
  3.2 0.1 select_reduce_fusion.2
  3.3 0.4 convert_reduce_fusion
  3.8 0.1 reduce_max.9
  3.9 1.3 compare_reduce_fusion
  5.8 0.8 copy.53
  6.6 1.0 reshape.162
  7.6 184.0 %conditional.1 = (bf16[2,128,256]{2,1,0:T(8,128)(2,1)S(1)}, bf16[4,4,1024]{2,1,0:T(4,128)(2,1)S(1)}) conditional(s32[]{:T(128)} %clamp.3, (s32[512,8]{0,1:T(8,128)}, s32[]{:T(128)}, s32[]{:T(128)}, s32[32]{0:T(128)}, s32[32,32]{1,0:T(8,128)S(1)}, /*index=5*/s32[2,32]{1,0:T(2,128)S(1)}, s32[1,32]{1,0:T(1,128)S(1)}, f32[512,8]{0,1:T(8,128)}, ...), branch_computations={%region_6.10_spmd.clone, %region_10.14_spmd.clone} | conditional | flops 7203 | bytes 330914 | solution.py:601
  7.6 0.7 broadcast_compare_fusion
  8.3 0.1 reduce_sum.94
  8.4 0.1 fusion
  8.5 0.8 constant_dynamic-slice_fusion
  9.3 0.8 constant_dynamic-slice_fusion.1
  10.1 0.1 select_reduce_fusion
  10.2 0.7 reshape.167.new
  10.9 0.8 copy.60
  11.7 0.1 broadcast_in_dim.114.gate
  11.8 179.6 %branch_0_fun.2 = (bf16[2,128,256]{2,1,0:T(8,128)(2,1)S(1)}, bf16[16,1024]{1,0:T(8,128)(2,1)S(1)}) custom-call(s32[2,97]{1,0:T(2,128)S(1)} %get-tuple-element.330.tbl, s32[4]{0:T(128)} %get-tuple-element.349.lens, f32[32,56,256]{2,1,0:T(8,128)} %get-tuple-element.350.master_hbm, bf16[512,1792]{1,0:T(8,128)(2,1)} %get-tuple-element.351.x_hbm, ...), custom_call_target="tpu_custom_call" | custom-call | tf_op jit(solution)/shard_map/cond/branch_0_fun/pallas_call | solution.py:491
  191.6 0.0 copy-start
  191.6 0.7 copy.67
  192.3 0.0 copy-done
  (10 shorter events, 0.1 us)
Async XLA Ops:
  191.6 0.7 copy-start

commit v2 on v1

--- a/solution.py
+++ b/solution.py
@@ -13,7 +13,7 @@
 GROUP = 8
 F32 = jnp.float32
 BF16 = jnp.bfloat16
-SPREADS = (3.2, None)
+SPREADS = (2.6, 3.8)
 
 
 def capacities(n, spread):
@@ -60,7 +60,8 @@
     lens,
     master_hbm,
     x_hbm,
-    gate,
+    routes,
+    route_weight,
     att,
     qn,
     qr,
@@ -84,6 +85,8 @@
         spread,
         weights,
         landed,
+        gate,
+        total,
         maps,
         qlat,
         probs,
@@ -140,7 +143,7 @@
     for step in range(1, heads):
         to = lax.rem(h + step, heads)
         copy = pltpu.make_async_remote_copy(
-            src_ref=att.at[to],
+            src_ref=att.at[:, pl.ds(pl.multiple_of(to * local_heads, local_heads), local_heads), :],
             dst_ref=landed.at[h],
             send_sem=head_send.at[step],
             recv_sem=head_recv.at[h],
@@ -153,7 +156,7 @@
     def head_arrival(step):
         source = lax.rem(h + step, heads)
         return pltpu.make_async_remote_copy(
-            src_ref=att.at[source],
+            src_ref=landed.at[h],
             dst_ref=landed.at[source],
             send_sem=head_send.at[step],
             recv_sem=head_recv.at[source],
@@ -205,21 +208,17 @@
     def attention():
         for step in range(1, heads):
             head_arrival(step).wait_recv()
-        landed[h] = att[h]
-        flat = landed[...].reshape(heads * att.shape[1], att.shape[2]).astype(BF16)
-        per = att.shape[1]
+        landed[h] = att[:, pl.ds(pl.multiple_of(h * local_heads, local_heads), local_heads), :]
+        per = att.shape[0] * local_heads
+        flat = landed[...].reshape(heads * per, 2 * hdim).astype(BF16)
+        row = lax.broadcasted_iota(jnp.int32, (block, heads * per), 0)
+        col = lax.broadcasted_iota(jnp.int32, (block, heads * per), 1)
         for hq in range(2):
-            for side in range(2):
-                row = lax.broadcasted_iota(jnp.int32, (block, heads * per), 0)
-                col = lax.broadcasted_iota(jnp.int32, (block, heads * per), 1)
-                want = (row >> 1) * per + hq * 4 + (row & 1) * 2 + side
-                pick = jnp.where(col == want, 1.0, 0.0).astype(BF16)
-                piece = jnp.dot(pick, flat, preferred_element_type=F32).astype(BF16)
-                maps[
-                    2 * y + hq,
-                    pl.ds(pl.multiple_of(z * block, block), block),
-                    side * hdim : (side + 1) * hdim,
-                ] = piece
+            want = (row >> 1) * per + (row & 1) * local_heads + 2 * y + hq
+            pick = jnp.where(col == want, 1.0, 0.0).astype(BF16)
+            maps[2 * y + hq, pl.ds(pl.multiple_of(z * block, block), block), :] = jnp.dot(
+                pick, flat, preferred_element_type=F32
+            ).astype(BF16)
         for hop in range(1, half + 2):
             for sign in (1, -1):
                 top = half if sign > 0 else half - 1
@@ -248,42 +247,50 @@
         y_copy(3, -1, 2 * y_far + 1, 1).wait_recv()
         loads[2].wait()
         yield
-        group = qn.shape[0]
+        total_rows = qn.shape[0]
+        group = total_rows // local_heads
+        order = lax.broadcasted_iota(jnp.int32, (total_rows, total_rows), 0)
+        order = (order & (group - 1)) * local_heads + (order >> (group.bit_length() - 1))
+        spot = lax.broadcasted_iota(jnp.int32, (total_rows, total_rows), 1)
+        pick = jnp.where(order == spot, 1.0, 0.0).astype(BF16)
+        q_all = jnp.dot(pick, qn[...], preferred_element_type=F32).astype(BF16)
+        q_rope = jnp.dot(pick, qr[...], preferred_element_type=F32).astype(BF16)
         contract = (((1,), (1,)), ((), ()))
         for head in range(local_heads):
-            q = qn[:, head * hdim : (head + 1) * hdim]
+            q = q_all[head * group : (head + 1) * group]
             qlat[head * group : (head + 1) * group, :] = lax.dot_general(
                 q, maps[head, :, :hdim], contract, preferred_element_type=F32
             ).astype(BF16)
         yield
-        total_rows = local_heads * group
         count, slots = cache.shape[0], cache.shape[2]
         scale = 1.0 / math.sqrt(hdim + qr.shape[1])
         row = lax.broadcasted_iota(jnp.int32, (total_rows, slots), 0) & (count - 1)
         col = lax.broadcasted_iota(jnp.int32, (total_rows, slots), 1)
-        score = jnp.full((total_rows, slots), -1e30, F32)
+        probs[...] = jnp.full((total_rows, slots), -1e30, F32)
         for r in range(count):
             part = jnp.dot(qlat[...], cache[r, :lat, :], preferred_element_type=F32) + jnp.dot(
-                qr[...], cache[r, lat:, :], preferred_element_type=F32
+                q_rope, cache[r, lat:, :], preferred_element_type=F32
             )
-            score = jnp.where((row == r) & (col < lens[r]), part * scale, score)
+            probs[...] = jnp.where((row == r) & (col < lens[r]), part * scale, probs[...])
+            yield
         fresh = lax.dot_general(
             qlat[...], new[:, :lat], contract, preferred_element_type=F32
-        ) + lax.dot_general(qr[...], new[:, lat:], contract, preferred_element_type=F32)
+        ) + lax.dot_general(q_rope, new[:, lat:], contract, preferred_element_type=F32)
         nrow = lax.broadcasted_iota(jnp.int32, fresh.shape, 0)
         ncol = lax.broadcasted_iota(jnp.int32, fresh.shape, 1)
         shift = count.bit_length() - 1
         same = (nrow & (count - 1)) == (ncol & (count - 1))
         step_of = (nrow >> shift) & (group // count - 1)
         fresh = jnp.where(same & ((ncol >> shift) <= step_of), fresh * scale, -1e30)
+        score = probs[...]
         top = jnp.maximum(
             jnp.max(score, axis=1, keepdims=True), jnp.max(fresh, axis=1, keepdims=True)
         )
         old_exp = jnp.exp(score - top)
         new_exp = jnp.exp(fresh - top)
-        total = jnp.sum(old_exp, axis=1, keepdims=True) + jnp.sum(new_exp, axis=1, keepdims=True)
-        probs[...] = old_exp / total
-        new_probs = (new_exp / total).astype(BF16)
+        mass = jnp.sum(old_exp, axis=1, keepdims=True) + jnp.sum(new_exp, axis=1, keepdims=True)
+        probs[...] = old_exp / mass
+        new_probs = (new_exp / mass).astype(BF16)
         latent[...] = jnp.dot(new_probs, new[:, :lat], preferred_element_type=F32)
         yield
         for r in range(count):
@@ -291,7 +298,7 @@
             latent[...] += lax.dot_general(
                 mine, cache[r, :lat, :], contract, preferred_element_type=F32
             )
-        yield
+            yield
         for head in range(local_heads):
             lh = latent[head * group : (head + 1) * group, :].astype(BF16)
             at_out[:, head * hdim : (head + 1) * hdim] = jnp.dot(
@@ -299,12 +306,17 @@
             ).astype(BF16)
 
     def widen():
+        weights[...] = jnp.zeros_like(weights)
         for slot in range(SLOTS):
             rank = jnp.clip(tbl[0, zn] + slot, 0, tbl.shape[1] - 1)
             expert = jnp.clip(tbl[1, rank], 0, master.shape[0] - 1)
             weights[slot, pl.ds(pl.multiple_of(z * pad_rows, pad_rows), rows), :] = master[
                 expert
             ].astype(BF16)
+            live = tbl[0, zn] + slot < tbl[0, zn + 1]
+            at = pl.ds(pl.multiple_of(y * share, share), share)
+            hit = jnp.where(routes[:, at] == jnp.where(live, expert, -1), route_weight[:, at], 0.0)
+            gate[slot] = jnp.broadcast_to(jnp.sum(hit, axis=0, keepdims=True), (lanes, share)).T
         loads[1].wait()
         yield
         row = lax.broadcasted_iota(jnp.int32, spread.shape, 0)
@@ -377,7 +389,6 @@
         )
 
     loads[0].wait()
-    weights[...] = jnp.zeros_like(weights)
     recent = {1: [], -1: []}
     side = [attention()]
     wider = [widen()]
@@ -422,7 +433,7 @@
 
     def partial(slot, target):
         at = pl.ds(pl.multiple_of(target * share, share), share)
-        return jnp.dot(wide_x[at, :], weights[slot], preferred_element_type=F32)
+        return total[slot, at, :]
 
     def rs_copy(index, sign):
         return pltpu.make_async_remote_copy(
@@ -440,6 +451,11 @@
         copy.start()
         open_sends.append(copy)
 
+    def multiply(slot, carry):
+        total[slot] = jnp.dot(wide_x[...], weights[slot], preferred_element_type=F32)
+        return carry
+
+    lax.fori_loop(0, SLOTS, multiply, 0)
     send_sum(0, 1, partial(0, y_far))
     send_sum(1, -1, partial(1, y_far))
     send_sum(2, 1, partial(1, y_to[1]))
@@ -465,7 +481,7 @@
 
 def exchange(sizes, caps, collective_id, operands):
     n, heads, reps = sizes
-    tbl, lens, master, x, gate, att, qn, qr, cache, new = operands
+    tbl, lens, master, x, routes, route_weight, att, qn, qr, cache, new = operands
     experts, rows, units = master.shape
     head_rows = rows * 4 // 7
     pad_rows = 1 << (rows - 1).bit_length()
@@ -473,9 +489,9 @@
     most = -(-max(caps) // GROUP)
     copies = 4 * (n // 2) * most
     lat = cache.shape[1] - qr.shape[1]
-    hdim = att.shape[2]
+    hdim = att.shape[2] // 2
     total_rows = qr.shape[0]
-    local_heads = qn.shape[1] // hdim
+    local_heads = att.shape[1] // heads
     share = x.shape[0] // reps
     group = n
     while group % 2 == 0 and group * rows // 2 % 128 == 0:
@@ -492,9 +508,9 @@
         functools.partial(body, n, heads, reps, caps),
         out_shape=(
             jax.ShapeDtypeStruct((SLOTS, share, units), BF16),
-            jax.ShapeDtypeStruct(qn.shape, BF16),
+            jax.ShapeDtypeStruct((total_rows // local_heads, local_heads * hdim), BF16),
         ),
-        in_specs=[smem, smem, hbm, hbm, vmem, vmem, vmem, vmem, hbm, vmem],
+        in_specs=[smem, smem, hbm, hbm, vmem, vmem, vmem, vmem, vmem, hbm, vmem],
         out_specs=(vmem, vmem),
         scratch_shapes=[pltpu.VMEM(shape, BF16) for shape in shapes]
         + [
@@ -504,7 +520,9 @@
             pltpu.VMEM((x.shape[0], n * pad_rows), BF16),
             pltpu.VMEM((group * rows, group * pad_rows), BF16),
             pltpu.VMEM((SLOTS, n * pad_rows, units), BF16),
-            pltpu.VMEM(att.shape, F32),
+            pltpu.VMEM((heads, att.shape[0], local_heads, 2 * hdim), F32),
+            pltpu.VMEM((SLOTS, share, units // 2), F32),
+            pltpu.VMEM((SLOTS, x.shape[0], units), F32),
             pltpu.VMEM((local_heads, lat, 2 * hdim), BF16),
             pltpu.VMEM((total_rows, lat), BF16),
             pltpu.VMEM((total_rows, cache.shape[2]), F32),
@@ -531,6 +549,102 @@
     )(*operands)
 
 
+def plain(
+    expert_master,
+    placement,
+    hidden_rows,
+    routes,
+    route_weight,
+    att_master,
+    query_nope,
+    query_rope,
+    cache_latent,
+    cache_len,
+    new_latent,
+):
+    owners = lax.axis_size("fsdp")
+    hdim = query_nope.shape[3]
+    query_lat = cache_latent.shape[2] - query_rope.shape[3]
+    count = placement.shape[0]
+    expert_ids = jnp.arange(count, dtype=jnp.int32)
+    same = placement[:, None] == placement[None, :]
+    earlier = expert_ids[None, :] < expert_ids[:, None]
+    slot_of = jnp.sum((same & earlier).astype(jnp.int32), axis=1)
+    owner_ids = jnp.arange(owners, dtype=jnp.int32)
+    slot_ids = jnp.arange(SLOTS, dtype=jnp.int32)
+    match = (slot_ids[:, None, None] == slot_of[None, None, :]) & (
+        owner_ids[None, :, None] == placement[None, None, :]
+    )
+    picked = jnp.sum(jnp.where(match, expert_ids[None, None, :], 0), axis=2)
+    filled = jnp.any(match, axis=2)
+    row_count = expert_master.shape[1]
+    unit_count = expert_master.shape[2]
+    mine = lax.axis_index("fsdp")
+    share_rows = hidden_rows.shape[0] // lax.axis_size("rep")
+    first_row = lax.axis_index("rep") * share_rows
+    blocks = jnp.take(expert_master, picked.reshape(-1), axis=0).astype(jnp.bfloat16)
+    blocks = blocks.reshape(SLOTS, owners, row_count, unit_count)
+    outgoing = jnp.where(filled[:, :, None, None], blocks, jnp.zeros_like(blocks))
+    arrived = lax.all_to_all(outgoing, "fsdp", split_axis=1, concat_axis=1, tiled=True)
+    weights_here = arrived.reshape(SLOTS, owners * row_count, unit_count)
+    my_experts = lax.dynamic_index_in_dim(picked, mine, 1, keepdims=False)
+    my_filled = lax.dynamic_index_in_dim(filled, mine, 1, keepdims=False)
+    terms = jnp.einsum("rd,sdf->srf", hidden_rows, weights_here, preferred_element_type=jnp.float32)
+    hits = routes[None, :, :] == my_experts[:, None, None]
+    gate = jnp.sum(jnp.where(hits, route_weight[None, :, :], 0.0), axis=2)
+    gate = jnp.where(my_filled[:, None], gate, 0.0)
+    shares = lax.all_to_all(terms, "rep", split_axis=1, concat_axis=0, tiled=True)
+    share = jnp.sum(shares.reshape(-1, SLOTS, share_rows, unit_count), axis=0)
+    gate_share = lax.dynamic_slice_in_dim(gate, first_row, share_rows, 1)
+    activated = (jax.nn.silu(share) * gate_share[:, :, None]).astype(jnp.bfloat16)
+    local_maps = att_master.astype(jnp.bfloat16)[None]
+    copies = jnp.broadcast_to(local_maps, (owners, *local_maps.shape[1:]))
+    widened = lax.all_to_all(copies, "fsdp", split_axis=0, concat_axis=0, tiled=True)
+    spread = lax.all_to_all(widened[:, None], "head", split_axis=3, concat_axis=1, tiled=True)
+    maps = spread.reshape(-1, spread.shape[3], spread.shape[4])
+    key_map = maps[:, :, :hdim]
+    value_map = maps[:, :, hdim:]
+    q_latent = jnp.einsum(
+        "trhd,lhd->trhl", query_nope, key_map, preferred_element_type=jnp.float32
+    ).astype(jnp.bfloat16)
+    query_full = jnp.concatenate([q_latent, query_rope], axis=3)
+    scale = 1.0 / math.sqrt(query_nope.shape[3] + query_rope.shape[3])
+    old_scores = (
+        jnp.einsum("trhc,rjc->trhj", query_full, cache_latent, preferred_element_type=jnp.float32)
+        * scale
+    )
+    new_scores = (
+        jnp.einsum("trhc,urc->trhu", query_full, new_latent, preferred_element_type=jnp.float32)
+        * scale
+    )
+    positions = jnp.arange(cache_latent.shape[1], dtype=jnp.int32)
+    live = positions[None, :] < cache_len[:, None]
+    old_scores = jnp.where(live[None, :, None, :], old_scores, -1e30)
+    step_ids = jnp.arange(new_latent.shape[0], dtype=jnp.int32)
+    causal = step_ids[None, :] <= step_ids[:, None]
+    new_scores = jnp.where(causal[:, None, None, :], new_scores, -1e30)
+    highest = jnp.maximum(jnp.max(old_scores, axis=3), jnp.max(new_scores, axis=3))
+    old_exp = jnp.exp(old_scores - highest[..., None])
+    new_exp = jnp.exp(new_scores - highest[..., None])
+    total = jnp.sum(old_exp, axis=3) + jnp.sum(new_exp, axis=3)
+    old_probs = (old_exp / total[..., None]).astype(jnp.bfloat16)
+    new_probs = (new_exp / total[..., None]).astype(jnp.bfloat16)
+    latent_full = jnp.einsum(
+        "trhj,rjc->trhc", old_probs, cache_latent, preferred_element_type=jnp.float32
+    )
+    latent_full = latent_full + jnp.einsum(
+        "trhu,urc->trhc", new_probs, new_latent, preferred_element_type=jnp.float32
+    )
+    latent_out = latent_full[..., :query_lat].astype(jnp.bfloat16)
+    attention = jnp.einsum(
+        "trhl,lhv->trhv", latent_out, value_map, preferred_element_type=jnp.float32
+    ).astype(jnp.bfloat16)
+    attention_out = attention.reshape(
+        attention.shape[0], attention.shape[1], attention.shape[2] * attention.shape[3]
+    )
+    return (activated, attention_out)
+
+
 def local(
     sizes,
     expert_master,
@@ -550,11 +664,10 @@
     count = placement.shape[0]
     ids = jnp.arange(count, dtype=jnp.int32)
     width = max(3 * n + 1, 3 * count)
-    turns = jnp.arange(3, dtype=jnp.int32) * n
     places = jnp.arange(width, dtype=jnp.int32)
-    below = jnp.sum(
-        ((placement[None, None, :] + turns[None, :, None]) < places[:, None, None]).astype(jnp.int32),
-        axis=(1, 2),
+    below = sum(
+        jnp.sum((placement[None, :] < (places - turn * n)[:, None]).astype(jnp.int32), axis=1)
+        for turn in range(3)
     )
     before = (placement[None, :] < placement[:, None]) | (
         (placement[None, :] == placement[:, None]) & (ids[None, :] < ids[:, None])
@@ -562,43 +675,49 @@
     rank = jnp.sum(before.astype(jnp.int32), axis=1)
     ordered = jnp.sum(jnp.where(rank[None, :] == places[:, None] % count, ids[None, :], 0), axis=1)
     tbl = jnp.stack([below, ordered])
-    slot_of = jnp.sum(
-        ((placement[:, None] == placement[None, :]) & (ids[None, :] < ids[:, None])).astype(jnp.int32), axis=1
-    )
-    slots = jnp.arange(SLOTS, dtype=jnp.int32)
-    here = (placement == z)[None, :] & (slot_of[None, :] == slots[:, None])
-    mine = jnp.sum(jnp.where(here, ids[None, :] + 1, 0), axis=1) - 1
-    share = hidden_rows.shape[0] // reps
-    my_routes = lax.dynamic_slice_in_dim(routes, y * share, share, 0)
-    my_weight = lax.dynamic_slice_in_dim(route_weight, y * share, share, 0)
-    gate = jnp.sum(jnp.where(my_routes[None] == mine[:, None, None], my_weight[None], 0.0), axis=2)
-    units = expert_master.shape[2]
-    gate = jnp.broadcast_to(gate[:, :, None], (SLOTS, share, units // 2))
-
-    lat_rows, all_heads, both = att_master.shape
-    local_heads = all_heads // heads
-    att = att_master.reshape(lat_rows, heads, reps, 2, 2, both // 2)
-    att = lax.dynamic_index_in_dim(att, y, 2, keepdims=False)
-    att = att.transpose(1, 2, 0, 3, 4).reshape(heads, lat_rows * 4, both // 2)
-
+    local_heads = att_master.shape[1] // heads
     steps, rows_here = query_nope.shape[0], query_nope.shape[1]
     group = steps * rows_here
-    qn = query_nope.reshape(group, -1)
-    qr = query_rope.reshape(group, local_heads, -1).transpose(1, 0, 2).reshape(group * local_heads, -1)
-    new = new_latent.reshape(group, -1)
-    operands = (tbl, cache_len, expert_master, hidden_rows, gate, att, qn, qr, jnp.swapaxes(cache_latent, 1, 2), new)
+    operands = (
+        tbl,
+        cache_len,
+        expert_master,
+        hidden_rows,
+        routes.T,
+        route_weight.T,
+        att_master,
+        query_nope.reshape(group * local_heads, -1),
+        query_rope.reshape(group * local_heads, -1),
+        jnp.swapaxes(cache_latent, 1, 2),
+        new_latent.reshape(group, -1),
+    )
 
     table = [capacities(n, spread) for spread in SPREADS]
     runs = jnp.arange(1, n // 2 + 1, dtype=jnp.int32)
     away = (placement[None, :] - jnp.arange(n, dtype=jnp.int32)[:, None] + n) % n
     held = jnp.sum((away[None] < runs[:, None, None]).astype(jnp.int32), axis=2)
     fullest = jnp.max(held, axis=1)
-    tier = jnp.int32(0)
-    for caps in table[:-1]:
-        over = jnp.any(fullest > jnp.asarray(caps[1:], jnp.int32))
-        tier = jnp.where(over & (tier == table.index(caps)), tier + 1, tier)
+    limits = jnp.asarray([caps[1:] for caps in table], jnp.int32)
+    tier = jnp.sum(jnp.any(fullest[None, :] > limits, axis=1).astype(jnp.int32))
     branches = [functools.partial(exchange, sizes, caps, index) for index, caps in enumerate(table)]
-    hidden, attended = lax.switch(tier, branches, operands)
+
+    def otherwise(_):
+        hidden, attended = plain(
+            expert_master,
+            placement,
+            hidden_rows,
+            routes,
+            route_weight,
+            att_master,
+            query_nope,
+            query_rope,
+            cache_latent,
+            cache_len,
+            new_latent,
+        )
+        return hidden, attended.reshape(group, -1)
+
+    hidden, attended = lax.switch(tier, [*branches, otherwise], operands)
     return hidden, attended.reshape(steps, rows_here, -1)
 
 

time: 193 us -> 182 us (0.943)
  the two profiles are of different devices: /device:TPU:32 before, /device:TPU:8 now
where the time goes in v2:
time: 182 us; the launch traced here: 181 us
  Pallas kernels  174 us (96%)
  other arithmetic  3.75 us (2%)
  local copies, waits for them, and re-layouts  2.35 us (1%)
    pallas_call x1, Pallas kernels, exchange(): pl.pallas_call(functools.partial(body, n, heads, reps, caps), out_shape=(...  174 us

profile of v2, /device:TPU:8, one launch (start us, length us, event | category | flops | bytes accessed | tf_op | source)
XLA Modules:
  0.0 181.5 jit_solution(12010375387653277659)
XLA Ops:
  0.6 0.7 convert_reduce_fusion.4
  1.4 0.9 convert_reduce_fusion.2
  2.3 0.1 select_reduce_fusion.1
  2.4 0.4 convert_reduce_fusion.1
  2.9 0.1 reduce_max.27
  3.0 0.8 compare_reduce_fusion
  3.8 0.6 convert_reduce_fusion.6
  5.1 174.8 %conditional.1 = (bf16[4,4,1024]{2,1,0:T(4,128)(2,1)S(1)}, bf16[2,128,256]{2,1,0:T(8,128)(2,1)}) conditional(s32[]{:T(128)} %clamp.3, (bf16[4,4,8,128]{3,2,1,0:T(8,128)(2,1)}, bf16[4,4,8,64]{3,2,1,0:T(8,128)(2,1)}, bf16[4,4,576]{2,1,0:T(4,128)(2,1)}, s32[2,97]{1,0:T(2,128)S(1)}, s32[4]{0:T(128)}, ...), branch_computations={%region_9.10_spmd, %region_10.11_spmd, %region_11.21_spmd} | conditional | flops 1128774144 | bytes 107511456 | solution.py:720
  5.1 0.7 reshape.253.new
  5.8 173.8 %branch_0_fun.1 = (bf16[2,128,256]{2,1,0:T(8,128)(2,1)}, bf16[16,1024]{1,0:T(8,128)(2,1)S(1)}) custom-call(s32[2,97]{1,0:T(2,128)S(1)} %get-tuple-element.77.tbl, s32[4]{0:T(128)} %get-tuple-element.78.lens, f32[32,56,256]{2,1,0:T(8,128)} %get-tuple-element.79.master_hbm, bf16[512,1792]{1,0:T(8,128)(2,1)} %get-tuple-element.80.x_hbm, ...), custom_call_target="tpu_custom_call" | custom-call | tf_op jit(solution)/shard_map/cond/branch_0_fun/pallas_call | solution.py:507
  179.9 0.0 copy-start.10
  179.9 1.6 copy.189
  181.4 0.0 copy-done.10
  (6 shorter events, 0.1 us)
Async XLA Ops:
  179.9 1.6 copy-start.10
